TPU v7x, 256 devices: a whole 4x4x8 slice. The times are simulated.
256 devices in a mesh: wide: 32 (over x, z), sib: 8 (over y, core).
Axes of the slice: x: 4, y: 4, z: 8, core: 2. Of those that a mesh axis runs over, the one named last changes fastest.
Arguments:
- points: bfloat16 [1048576, 128], P(('wide', 'sib')), may hold values from -40 to 40
- charges: bfloat16 [1048576, 128], P(('wide', 'sib')), may hold values from -2.5 to 2.5
- skel: int32 [4096, 128], P(('wide', 'sib')), may hold values from 0 to 255, all different within a row
- near_list: int32 [4096, 6], P(('wide', 'sib')), may hold values from 0 to 15, all different within a row
- far_gap: int32 [4096, 4], P(('wide', 'sib')), may hold values from 0 to 30, all different within a row; in each aligned block of 16 rows (0 to 15, 16 to 31, ...) at most 5 rows name the same one
- far_leaf: int32 [4096, 4], P(('wide', 'sib')), may hold values from 0 to 15
- par_pick: int32 [4096, 64], P(('wide', 'sib')), may hold values from 0 to 127, all different within a row
Outputs:
- potential: bfloat16 [1048576, 128], P(('wide', 'sib'))
- transfer: float32 [4096, 128, 128], P(('wide', 'sib'))
Inputs may be any that keep to these rules, and one draw needn't show every extreme that they name: `skel`: the 128 numbers of a row are distinct. `near_list`: the 6 numbers of a row are distinct. `far_gap`: the 4 offsets of a row are distinct; over the rows of one device no offset appears more than 5 times, and some offset appears exactly 5 times. `par_pick`: the 64 numbers of a row are distinct.
All inputs are finite; a program needn't handle non-finite values.
Results may differ from a plain program's by a relative error of at most 0.0059.
Values may be sent and summed in bfloat16 or wider, within the bound.
A program may use at most 128 MiB of HBM per device.

v0:
```python
import math

import jax
import jax.numpy as jnp
from jax import lax
from jax.sharding import PartitionSpec as P

kernel_rate = 1.5


def partner(value, axis, apart):
    return lax.ppermute(value, axis, [(i, i ^ 1 << apart) for i in range(lax.axis_size(axis))])


def kernel_block(left_pts, right_pts):
    left_wide = left_pts.astype(jnp.float32)
    right_wide = right_pts.astype(jnp.float32)
    left_sq = jnp.sum(left_wide * left_wide, axis=-1)
    right_sq = jnp.sum(right_wide * right_wide, axis=-1)
    inner_prod = jnp.einsum(
        "...nd,...md->...nm", left_pts, right_pts, preferred_element_type=jnp.float32
    )
    sq_dist = left_sq[..., :, None] + right_sq[..., None, :] - 2.0 * inner_prod
    return jnp.exp(-kernel_rate * sq_dist / left_pts.shape[-1])


def gram_of(block):
    return jnp.einsum("lab,lac->lbc", block, block, precision=lax.Precision.HIGHEST)


def body(points, charges, skel, near_list, far_gap, far_leaf, par_pick):
    leaves = skel.shape[0]
    skel_rank = skel.shape[1]
    leaf_rows = points.shape[0] // leaves
    feature_dim = points.shape[1]
    target_cols = charges.shape[1]
    near_count = near_list.shape[1]
    far_count = far_gap.shape[1]
    leaf_pts = points.reshape(leaves, leaf_rows, feature_dim)
    leaf_chg = charges.reshape(leaves, leaf_rows, target_cols)
    skel_pts = jnp.take_along_axis(leaf_pts, skel[:, :, None], axis=1)
    leaf_bases = kernel_block(leaf_pts, skel_pts).astype(jnp.bfloat16)
    compressed = jnp.einsum(
        "lpr,lpc->lrc", leaf_bases, leaf_chg, preferred_element_type=jnp.float32
    ).astype(jnp.bfloat16)

    def near_block(operands):
        block_pts, near_ids = operands
        pair_count = near_ids.shape[0]
        near_pts = leaf_pts[near_ids].reshape(pair_count, near_count * leaf_rows, feature_dim)
        near_chg = leaf_chg[near_ids].reshape(pair_count, near_count * leaf_rows, target_cols)
        near_tiles = kernel_block(block_pts, near_pts).astype(jnp.bfloat16)
        return jnp.einsum("lpm,lmc->lpc", near_tiles, near_chg, preferred_element_type=jnp.float32)

    near_sum = lax.map(
        near_block,
        (
            leaf_pts.reshape(leaves // 2, 2, leaf_rows, feature_dim),
            near_list.reshape(leaves // 2, 2, near_count),
        ),
    )
    near_sum = near_sum.reshape(leaves, leaf_rows, target_cols)
    column = lax.axis_index("wide")
    wide_count = lax.axis_size("wide")
    peer_ids = (column + 1 + far_gap) % wide_count
    capacity = max(2, min(leaves, (2 * leaves * far_count + wide_count - 2) // (wide_count - 1)))
    flat_peer = peer_ids.reshape(-1)
    flat_leaf = far_leaf.reshape(-1)
    onehot = (flat_peer[:, None] == jnp.arange(wide_count, dtype=jnp.int32)[None, :]).astype(
        jnp.int32
    )
    before = jnp.cumsum(onehot, axis=0) - onehot
    slot_pos = jnp.sum(before * onehot, axis=1)
    wanted = jnp.zeros((wide_count, capacity), jnp.int32).at[flat_peer, slot_pos].set(flat_leaf)
    asked_ids = lax.all_to_all(wanted, "wide", split_axis=0, concat_axis=0, tiled=True)
    got_pts = lax.all_to_all(skel_pts[asked_ids], "wide", split_axis=0, concat_axis=0, tiled=True)
    got_q = lax.all_to_all(compressed[asked_ids], "wide", split_axis=0, concat_axis=0, tiled=True)
    far_pts = got_pts[flat_peer, slot_pos].reshape(leaves, far_count, skel_rank, feature_dim)
    far_q = got_q[flat_peer, slot_pos].reshape(leaves, far_count, skel_rank, target_cols)
    coupling = kernel_block(jnp.broadcast_to(skel_pts[:, None], far_pts.shape), far_pts).astype(
        jnp.bfloat16
    )
    gathered = jnp.einsum(
        "lkab,lkbc->lac", coupling, far_q, preferred_element_type=jnp.float32
    ).astype(jnp.bfloat16)
    summed = near_sum + jnp.einsum(
        "lpr,lrc->lpc", leaf_bases, gathered, preferred_element_type=jnp.float32
    )
    potential = summed.astype(jnp.bfloat16).reshape(leaves * leaf_rows, target_cols)
    own_half = jnp.take_along_axis(skel_pts, par_pick[:, :, None], axis=1)
    odd_side = lax.axis_index("sib") % 2 == 1
    other_pts, other_half = partner((skel_pts, own_half), "sib", 0)
    parent = jnp.where(
        odd_side,
        jnp.concatenate([other_half, own_half], axis=1),
        jnp.concatenate([own_half, other_half], axis=1),
    )
    own_block = kernel_block(skel_pts, parent)
    own_gram = gram_of(own_block)
    other_gram = gram_of(kernel_block(other_pts, parent))
    gram_sum = own_gram + other_gram + jnp.eye(skel_rank, dtype=jnp.float32)
    lower = jnp.linalg.cholesky(gram_sum)
    transfer = math.sqrt(2 * skel_rank) * lax.linalg.triangular_solve(
        lower, own_block, left_side=False, lower=True, transpose_a=True
    )
    return (potential, transfer)


def solution(mesh):
    placed = (
        P(("wide", "sib"), None),
        P(("wide", "sib"), None),
        P(("wide", "sib"), None),
        P(("wide", "sib"), None),
        P(("wide", "sib"), None),
        P(("wide", "sib"), None),
        P(("wide", "sib"), None),
    )
    return jax.shard_map(
        body,
        mesh=mesh,
        in_specs=placed,
        out_specs=(P(("wide", "sib"), None), P(("wide", "sib"), None, None)),
        check_vma=False,
    )
```

profile of v0, /device:TPU:14, one launch (start us, length us, event | category | flops | bytes accessed | tf_op | source)
XLA Modules:
  0.0 613.2 jit_solution(1386856871581574192)
XLA Ops:
  0.6 0.8 add_select_fusion
  2.0 0.8 copy.50
  2.9 3.5 scatter_fusion
  7.1 11.6 %all-to-all-start = ((s32[32,1,5]{2,1,0:T(1,128)}), s32[32,1,5]{2,1,0:T(1,128)S(1)}, u32[]{:S(2)}, u32[]{:S(2)}) async-start(s32[32,1,5]{2,1,0:T(1,128)} %copy.51), calls=%async_computation | async-start | bytes 32768 | tf_op jit(solution)/shard_map/all_to_all | solution.py:75
  18.7 0.7 fusion.37
  20.1 11.1 %gather_fusion.6 = bf16[2048,128]{1,0:T(8,128)(2,1)S(1)} fusion(bf16[16,256,128]{2,1,0:T(8,128)(2,1)S(1)} %bitcast.112, s32[2048]{0:T(1024)S(1)} %fusion.37), kind=kCustom, calls=%fused_computation.6 | custom fusion | bytes 1064960 | tf_op jit(solution)/shard_map/jit(take_along_axis)/gather | solution.py:41
  32.0 7.7 %gather_fusion.2 = bf16[160,128,128]{2,1,0:T(8,128)(2,1)} fusion(bf16[16,128,128]{2,1,0:T(8,128)(2,1)S(1)} %get-tuple-element.95, s32[1024]{0:T(1024)S(1)} %pad_clamp_fusion.1), kind=kCustom, calls=%fused_computation.2 | custom fusion | bytes 10486400 | tf_op jit(solution)/shard_map/gather | solution.py:76
  39.7 9.8 %all-to-all-start.1 = ((bf16[32,5,128,128]{3,2,1,0:T(8,128)(2,1)}), bf16[32,5,128,128]{3,2,1,0:T(8,128)(2,1)}, u32[]{:S(2)}, u32[]{:S(2)}) async-start(bf16[32,5,128,128]{3,2,1,0:T(8,128)(2,1)} %bitcast.124), calls=%async_computation.1 | async-start | bytes 10485760 | tf_op jit(solution)/shard_map/all_to_all | solution.py:76
  50.9 1.0 copy-done.2
  52.3 7.7 %gather_fusion.4 = bf16[160,128,128]{2,1,0:T(8,128)(2,1)} fusion(bf16[16,128,128]{2,1,0:T(8,128)(2,1)S(1)} %convolution_convert_fusion, s32[1024]{0:T(1024)S(1)} %pad_clamp_fusion.1), kind=kCustom, calls=%fused_computation.4 | custom fusion | bytes 10486400 | tf_op jit(solution)/shard_map/gather | solution.py:77
  60.1 105.9 %all-to-all-done.1 = bf16[32,5,128,128]{3,2,1,0:T(8,128)(2,1)} async-done(((bf16[32,5,128,128]{3,2,1,0:T(8,128)(2,1)}), bf16[32,5,128,128]{3,2,1,0:T(8,128)(2,1)}, u32[]{:S(2)}, u32[]{:S(2)}) %all-to-all-start.1) | async-done | bytes 5242912 | tf_op jit(solution)/shard_map/all_to_all | solution.py:76
  165.9 8.8 %all-to-all-start.2 = ((bf16[32,5,128,128]{3,2,1,0:T(8,128)(2,1)}), bf16[32,5,128,128]{3,2,1,0:T(8,128)(2,1)}, u32[]{:S(2)}, u32[]{:S(2)}) async-start(bf16[32,5,128,128]{3,2,1,0:T(8,128)(2,1)} %bitcast.123), calls=%async_computation.2 | async-start | bytes 10485760 | tf_op jit(solution)/shard_map/all_to_all | solution.py:77
  175.0 5.8 gather_fusion.7
  180.8 0.9 broadcast_select_fusion.1
  182.3 48.8 %while.12 = (s32[]{:T(128)}, f32[8,2,256,128]{3,2,1,0:T(8,128)}, bf16[8,2,256,128]{3,2,1,0:T(8,128)(2,1)S(1)}, s32[8,2,6]{2,1,0:T(2,128)S(1)}, bf16[16,256,128]{...) while((s32[]{:T(128)}, f32[8,2,256,128]{3,2,1,0:T(8,128)}, ...), condition=%wide.region_3.4_spmd, body=%wide.region_0.3_spmd.sunk | while | flops 407959072 | bytes 6088101 | solution.py:55
  183.6 1.6 gather_fusion
  185.3 3.1 fusion.69
  189.7 1.6 gather_fusion
  191.4 3.1 fusion.69
  195.8 1.6 gather_fusion
  197.5 3.1 fusion.69
  201.9 1.6 gather_fusion
  203.6 3.1 fusion.69
  208.0 1.6 gather_fusion
  209.7 3.1 fusion.69
  214.1 1.6 gather_fusion
  215.8 3.1 fusion.69
  220.2 1.6 gather_fusion
  221.9 3.1 fusion.69
  226.3 1.6 gather_fusion
  228.0 3.1 fusion.69
  231.3 1.6 multiply_reduce_fusion.4
  232.9 1.8 fusion.26
  234.7 1.9 fusion.44
  236.5 1.9 convolution_multiply_fusion.2
  238.4 1.4 fusion.23
  239.9 3.1 broadcast_add_fusion
  243.0 1.6 copy.58
  244.6 2.4 fusion.30
  247.0 188.3 %custom-call.7 = f32[16,128,128]{2,1,0:T(8,128)S(1)} custom-call(f32[16,128,128]{2,1,0:T(8,128)} %fusion.30), custom_call_target="Cholesky" | custom-call | tf_op jit(solution)/shard_map/jit(cholesky)/cholesky | solution.py:102
  435.5 1.2 select_bitcast_fusion
  436.6 157.9 %custom-call.8 = f32[16,1,128,128]{2,3,1,0:T(8,128)S(1)} custom-call(f32[16,1,128,128]{3,2,1,0:T(8,128)} %select_bitcast_fusion), custom_call_target="InvertDiagBlocksLowerTriangular" | custom-call | tf_op jit(solution)/shard_map/triangular_solve | solution.py:103
  594.6 2.2 convolution_multiply_fusion.1
  596.8 3.4 gather_fusion.3
  600.2 1.2 multiply_reduce_fusion.2
  601.4 4.7 gather_fusion.5
  606.0 3.7 fusion.27
  609.8 3.4 fusion.19
  (102 shorter events, 17.1 us)
Async XLA Ops:
  0.6 19.5 %copy-start = (bf16[4096,128]{1,0:T(8,128)(2,1)S(1)}, bf16[4096,128]{1,0:T(8,128)(2,1)}, u32[]{:S(2)}) copy-start(bf16[4096,128]{1,0:T(8,128)(2,1)} %param.9) | copy-start | bytes 3145732
  7.1 24.8 %all-to-all-start = ((s32[32,1,5]{2,1,0:T(1,128)}), s32[32,1,5]{2,1,0:T(1,128)S(1)}, u32[]{:S(2)}, u32[]{:S(2)}) async-start(s32[32,1,5]{2,1,0:T(1,128)} %copy.51), calls=%async_computation | async-start | bytes 32768 | tf_op jit(solution)/shard_map/all_to_all | solution.py:75
  39.7 126.2 %all-to-all-start.1 = ((bf16[32,5,128,128]{3,2,1,0:T(8,128)(2,1)}), bf16[32,5,128,128]{3,2,1,0:T(8,128)(2,1)}, u32[]{:S(2)}, u32[]{:S(2)}) async-start(bf16[32,5,128,128]{3,2,1,0:T(8,128)(2,1)} %bitcast.124), calls=%async_computation.1 | async-start | bytes 10485760 | tf_op jit(solution)/shard_map/all_to_all | solution.py:76
  50.2 1.7 copy-start.1
  50.9 1.0 copy-start.2
  165.9 8.9 %copy-start.3 = (s32[16,64]{1,0:T(8,128)S(1)}, s32[16,64]{1,0:T(8,128)}, u32[]{:S(2)}) copy-start(s32[16,64]{1,0:T(8,128)} %param.15) | copy-start | bytes 12292
  165.9 435.4 %all-to-all-start.2 = ((bf16[32,5,128,128]{3,2,1,0:T(8,128)(2,1)}), bf16[32,5,128,128]{3,2,1,0:T(8,128)(2,1)}, u32[]{:S(2)}, u32[]{:S(2)}) async-start(bf16[32,5,128,128]{3,2,1,0:T(8,128)(2,1)} %bitcast.123), calls=%async_computation.2 | async-start | bytes 10485760 | tf_op jit(solution)/shard_map/all_to_all | solution.py:77
  174.8 7.4 %copy-start.4 = (s32[16,6]{0,1:T(8,128)S(1)}, s32[16,6]{0,1:T(8,128)}, u32[]{:S(2)}) copy-start(s32[16,6]{0,1:T(8,128)} %param.12) | copy-start | bytes 1156
  174.8 61.7 %collective-permute-start.1 = (bf16[16,128,128]{2,1,0:T(8,128)(2,1)S(1)}, bf16[16,128,128]{2,1,0:T(8,128)(2,1)}, u32[]{:S(2)}, u32[]{:S(2)}) collective-permute-start(bf16[16,128,128]{2,1,0:T(8,128)(2,1)S(1)} %get-tuple-element.95), channel_id=1, source_target_pairs={{0,1},{1,0},{2,3},{3,2},{4,5},{5,4},{6,7},{7,6},{8,9},{9,8},{10,11... | collective-permute-start | bytes 1572872 | tf_op jit(solution)/shard_map/ppermute | solution.py:12
  181.7 49.5 %collective-permute-start = (bf16[16,64,128]{2,1,0:T(8,128)(2,1)}, bf16[16,64,128]{2,1,0:T(8,128)(2,1)}, u32[]{:S(2)}, u32[]{:S(2)}) collective-permute-start(bf16[16,64,128]{2,1,0:T(8,128)(2,1)} %broadcast_select_fusion.1), channel_id=1, source_target_pairs={{0,1},{1,0},{2,3},{3,2},{4,5},{5,4},{6,7},{7,6},{8,9},{9,8},{10,11... | collective-permute-start | bytes 786440 | tf_op jit(solution)/shard_map/ppermute | solution.py:12
where the time goes:
time: 615 us; the launch traced here: 613 us
  other arithmetic  364 us (59%)
  waiting for transfers between devices  106 us (17%)
  local copies, waits for them, and re-layouts  67.5 us (11%)
  matrix products  43.7 us (7%)
  starting transfers between devices  30.8 us (5%)
    another operation x4, other arithmetic, body(): lower = jnp.linalg.cholesky(gram_sum)  189 us
    another operation x3, other arithmetic, body(): lax.linalg.triangular_solve(lower, own_block, left_side=False, lower=True...  159 us
    all_to_all x1, waiting for transfers between devices, body(): lax.all_to_all(skel_pts[asked_ids], 'wide', split_axis=0, concat_axis=0,...  106 us
    dot_general x8, matrix products, near_block(): jnp.einsum('lpm,lmc->lpc', near_tiles, near_chg, preferred_element_type=j...  24.7 us
    gather x8, local copies, waits for them, and re-layouts, near_block(): leaf_chg[near_ids].reshape(pair_count, near_count * leaf_rows, target_cols)  12.4 us
  transfers between devices with their start and end apart: 5, of which 1 were waited for; matrix products, arithmetic and copies ran while one was open for 73% of the time, Pallas kernels for 0%

commit v1 on v0

v1 whole, which is shorter than its diff:
```python
import functools
import math

import jax
import jax.numpy as jnp
from jax import lax
from jax.experimental import pallas as pl
from jax.experimental.pallas import tpu as pltpu
from jax.sharding import PartitionSpec as P

F32, BF16 = jnp.float32, jnp.bfloat16
RATE = 2.0 * 1.5 / 128 / math.log(2.0)
NN = (((1,), (0,)), ((), ()))
NT = (((1,), (1,)), ((), ()))
TN = (((0,), (0,)), ((), ()))
MESH = pl.DeviceIdType.MESH

LEAVES, HALF = 16, 8
XN, ZN = 4, 8
PANEL = 32
CHUNKS = 7
UP = [(0, 0), (0, 1), (7, 0), (7, 1), (6, 0), (6, 1), (5, 0)]
DOWN = [(0, 1), (0, 0), (1, 1), (1, 0), (2, 1), (2, 0), (3, 1)]


def mm(a, b, dims=NN):
    return lax.dot_general(a, b, dims, preferred_element_type=F32)


def squares(pts):
    wide = pts.astype(F32)
    sq = wide * wide
    high = sq.astype(BF16)
    return high, (sq - high.astype(F32)).astype(BF16)


def half_col(pts):
    high, low = squares(pts)
    ones = jnp.ones((128, 128), BF16)
    return -0.5 * (mm(high, ones) + mm(low, ones))


def half_rows(pts):
    high, low = squares(pts)
    ones = jnp.ones((16, 128), BF16)
    return (-0.5 * (mm(ones, high, NT) + mm(ones, low, NT)))[0:8]


def kernel_exp(inner, col, row):
    return jnp.exp2(RATE * (inner + (col + row)))


def three(x):
    a = x.astype(BF16)
    rest = x - a.astype(F32)
    b = rest.astype(BF16)
    return a, b, (rest - b.astype(F32)).astype(BF16)


def pick_rows(index_row, pts):
    place = lax.broadcasted_iota(jnp.int32, (pts.shape[0], index_row.shape[1]), 0)
    hot = jnp.where(place == index_row, 1.0, 0.0).astype(BF16)
    return mm(hot, pts, TN).astype(BF16)


def near_prepare(x_ref, left_ref, right_ref, g):
    pts = x_ref[g]
    n1, n2, n3 = three(half_col(pts))
    lane = lax.broadcasted_iota(jnp.int32, pts.shape, 1)
    one, zero = jnp.ones(pts.shape, BF16), jnp.zeros(pts.shape, BF16)

    def parts(at):
        rest = jnp.where(lane == at + 2, n3, zero)
        return jnp.where(lane == at, n1, jnp.where(lane == at + 1, n2, rest))

    left_ref[g, :, 0:128] = pts
    right_ref[g, :, 0:128] = pts
    left_ref[g, :, 128:256] = jnp.where((lane >= 3) & (lane < 6), one, parts(0))
    right_ref[g, :, 128:256] = jnp.where(lane < 3, one, parts(3))


def near_leaf(left_ref, right_ref, c_ref, near_ref, g):
    left = left_ref[g]
    total = None
    for k in range(near_ref.shape[1]):
        m = near_ref[g, k]
        tile = jnp.exp2(RATE * mm(left, right_ref[m], NT)).astype(BF16)
        term = mm(tile, c_ref[m])
        total = term if total is None else total + term
    return total


def build_parent(w_ref, m, sa, sb, pa, pb):
    par = jnp.concatenate([pick_rows(pa, sa), pick_rows(pb, sb)], axis=0)
    col = half_col(par)
    ea = kernel_exp(mm(par, sa, NT), col, half_rows(sa)[0:1])
    eb = kernel_exp(mm(par, sb, NT), col, half_rows(sb)[0:1])
    both = jnp.concatenate([ea, eb], axis=1)
    gram = lax.dot_general(
        both, both, NT, precision=lax.Precision.HIGHEST, preferred_element_type=F32
    )
    row = lax.broadcasted_iota(jnp.int32, (128, 128), 0)
    lane = lax.broadcasted_iota(jnp.int32, (128, 128), 1)
    w_ref[m, :, 0:128] = gram + jnp.where(row == lane, 1.0, 0.0)
    w_ref[m, :, 128:384] = both


def factor_panel(w_ref, p):
    r0, b, n = p * PANEL, PANEL, w_ref.shape[0]
    lane = lax.broadcasted_iota(jnp.int32, (1, b, 128), 2)
    row = lax.broadcasted_iota(jnp.int32, (1, b, 128), 1)
    slab = w_ref[:, r0 : r0 + b, 0:128]
    if r0:
        slab = pltpu.roll(slab, 128 - r0, 2)
    a = jnp.where(lane < b, slab, jnp.where(lane == row + b, 1.0, 0.0))
    diag = jnp.zeros((n, b, 128), F32)
    for j in range(b):
        col = jnp.broadcast_to(a[:, :, j : j + 1], (n, b, 128))
        piv = col[:, j : j + 1, :]
        top = a[:, j : j + 1, :] / piv
        diag = jnp.where(row == j, piv, diag)
        a = a - jnp.where(row > j, col, 0.0) * top
    root = lax.rsqrt(diag)
    root = root * (1.5 - 0.5 * diag * root * root)
    inv = pltpu.roll(jnp.where(lane < 2 * b, a, 0.0) * root, 128 - b, 2)
    for m in range(n):
        l1, l2, l3 = three(inv[m][:, 0:b])
        left = jnp.concatenate([l1, l1, l2, l2, l1, l3], axis=1)
        r1, r2, r3 = three(w_ref[m, r0 : r0 + b, :])
        right = jnp.concatenate([r1, r2, r1, r2, r3, r1], axis=0)
        done = mm(left, right)
        w_ref[m, r0 : r0 + b, :] = done
        if r0 + b < 128:
            d1, d2, d3 = three(done)
            right = jnp.concatenate([d1, d2, d1, d2, d3, d1], axis=0)
            left = jnp.concatenate([d1, d1, d2, d2, d1, d3], axis=0)[:, 0:128]
            change = mm(left, right, TN)
            w_ref[m, r0 + b : 128, :] -= change[r0 + b : 128]


def kernel(
    x_ref, c_ref, skel_ref, near_ref, codes_ref, pick_ref,
    pot_ref, transfer_ref,
    sf, qf, sg, lists, list_sm, sib_s, sib_pick, left, right, basis, near_sum,
    norms, tiles, h_out, h_in, h_own, w, t_keep, t_send, t_recv,
    s_send, s_recv, q_send, q_recv, x_send, x_recv, h_send, h_recv,
    l_send, l_recv, b_send, b_recv, local_sem,
):
    wide, sib = lax.axis_index("wide"), lax.axis_index("sib")
    x, z = wide // ZN, wide % ZN
    odd = sib % 2
    above, below = (x * ZN + (z + 1) % ZN, sib), (x * ZN + (z + ZN - 1) % ZN, sib)
    peers = [None] + [((x + d) % XN * ZN + z, sib) for d in range(1, XN)]
    twin = (wide, sib + 1 - 2 * odd)

    barrier = pltpu.get_barrier_semaphore()
    for other in (above, below, *peers[1:], twin):
        pl.semaphore_signal(barrier, inc=1, device_id=other, device_id_type=MESH)

    def remote(src, dst, send, recv, device):
        return pltpu.make_async_remote_copy(
            src_ref=src, dst_ref=dst, send_sem=send, recv_sem=recv,
            device_id=device, device_id_type=MESH,
        )

    def ring(buf, send, recv):
        pairs = []
        for i in range(CHUNKS):
            pair = []
            for way, (plan, device, step) in enumerate(((UP, above, ZN - 1), (DOWN, below, 1))):
                slot, half = plan[i]
                rows = pl.ds(half * HALF, HALF)
                pair.append(
                    remote(
                        buf.at[slot, rows], buf.at[(slot + step) % ZN, rows],
                        send.at[way, i], recv.at[way, i], device,
                    )
                )
            pairs.append(pair)
        return pairs

    s_ring, q_ring = ring(sf, s_send, s_recv), ring(qf, q_send, q_recv)
    x_copies = [
        remote(sf.at[0], sg.at[XN - d], x_send.at[d], x_recv.at[XN - d], peers[d])
        for d in range(1, XN)
    ]
    x_arrivals = [
        remote(sf.at[0], sg.at[d], x_send.at[d], x_recv.at[d], peers[d]) for d in range(1, XN)
    ]
    l_copies = [
        remote(codes_ref, lists.at[XN - d], l_send.at[d], l_recv.at[XN - d], peers[d])
        for d in range(1, XN)
    ]
    l_arrivals = [
        remote(codes_ref, lists.at[d], l_send.at[d], l_recv.at[d], peers[d]) for d in range(1, XN)
    ]
    h_copies = [
        remote(h_out.at[d], h_in.at[XN - d], h_send.at[d], h_recv.at[XN - d], peers[d])
        for d in range(1, XN)
    ]
    h_arrivals = [
        remote(h_out.at[d], h_in.at[d], h_send.at[d], h_recv.at[d], peers[d]) for d in range(1, XN)
    ]
    mine, theirs = odd * HALF, HALF - odd * HALF
    pick_copy = remote(pick_ref, sib_pick, b_send.at[0], b_recv.at[0], twin)
    sib_copy = remote(sf.at[0, pl.ds(theirs, HALF)], sib_s, b_send.at[1], b_recv.at[1], twin)
    t_copy = remote(t_send, t_recv, b_send.at[2], b_recv.at[2], twin)

    def forward(copies, i):
        for way in (0, 1):
            copies[i - 2][way].wait_recv()
            copies[i][way].start()

    def skeleton(g):
        sf[0, g] = pick_rows(skel_ref[pl.ds(g, 1), :], x_ref[g])

    @pl.loop(0, HALF // 2)
    def _(i):
        skeleton(2 * i)
        skeleton(2 * i + 1)

    pl.semaphore_wait(barrier, 6)
    s_ring[0][0].start()
    s_ring[1][1].start()
    pick_copy.start()
    for copy in l_copies:
        copy.start()

    @pl.loop(HALF // 2, HALF)
    def _(i):
        skeleton(2 * i)
        skeleton(2 * i + 1)

    s_ring[0][1].start()
    s_ring[1][0].start()
    sib_copy.start()
    for copy in x_copies:
        copy.start()

    def compress(g):
        pts, skel_pts = x_ref[g], sf[0, g]
        block = kernel_exp(mm(pts, skel_pts, NT), half_col(pts), half_rows(skel_pts)[0:1])
        block = block.astype(BF16)
        basis[g] = block
        qf[0, g] = mm(block, c_ref[g], TN).astype(BF16)

    def bases(first, last):
        @pl.loop(first // 2, last // 2)
        def _(i):
            compress(2 * i)
            compress(2 * i + 1)

    bases(0, 8)
    forward(s_ring, 2)
    bases(8, 16)
    forward(s_ring, 3)
    for i in (0, 1):
        for way in (0, 1):
            q_ring[i][way].start()

    @pl.loop(0, LEAVES)
    def _(g):
        near_prepare(x_ref, left, right, g)

    def near(first, last):
        @pl.loop(first, last)
        def _(g):
            near_sum[g] = near_leaf(left, right, c_ref, near_ref, g)

    near(0, 4)
    forward(s_ring, 4)
    near(4, 8)
    forward(q_ring, 2)
    near(8, 12)
    forward(s_ring, 5)
    near(12, 16)
    forward(q_ring, 3)

    pick_copy.wait_recv()
    sib_copy.wait_recv()

    @pl.loop(0, HALF // 2)
    def _(i):
        for m in (2 * i, 2 * i + 1):
            own, other = sf[0, mine + m], sib_s[m]
            own_pick = pick_ref[pl.ds(mine + m, 1), 0:64]
            other_pick = sib_pick[pl.ds(mine + m, 1), 0:64]
            build_parent(
                w, m,
                jnp.where(odd == 1, other, own), jnp.where(odd == 1, own, other),
                jnp.where(odd == 1, other_pick, own_pick),
                jnp.where(odd == 1, own_pick, other_pick),
            )

    forward(s_ring, 6)
    factor_panel(w, 0)
    forward(q_ring, 4)
    factor_panel(w, 1)
    factor_panel(w, 2)
    forward(q_ring, 5)
    factor_panel(w, 3)

    @pl.loop(0, HALF)
    def _(m):
        ta = w[m, :, 128:256].T * 16.0
        tb = w[m, :, 256:384].T * 16.0
        t_keep[m] = jnp.where(odd == 1, tb, ta)
        t_send[m] = jnp.where(odd == 1, ta, tb)

    t_copy.start()
    keep_copy = pltpu.make_async_copy(t_keep, transfer_ref.at[pl.ds(mine, HALF)], local_sem.at[0])
    keep_copy.start()

    for copy in l_arrivals:
        copy.wait_recv()
    list_copies = [
        pltpu.make_async_copy(codes_ref if d == 0 else lists.at[d], list_sm.at[d], local_sem.at[1 + d])
        for d in range(XN)
    ]
    for copy in list_copies:
        copy.start()
    for i in (5, 6):
        for way in (0, 1):
            s_ring[i][way].wait_recv()
    for copy in x_arrivals:
        copy.wait_recv()
    for copy in list_copies:
        copy.wait()

    @pl.loop(0, ZN * LEAVES // 4)
    def _(i):
        for f in range(4):
            norms[4 * i + f] = half_rows(sf[i // 4, i % 4 * 4 + f])

    def entry(d, g, k):
        code = list_sm[d, 0, g * 4 + k]
        ahead = 1 + (code >> 4)
        there = ((z + ahead >> 3) + d & XN - 1) == 0
        return there, (ahead & ZN - 1) * LEAVES + (code & LEAVES - 1)

    def couple(d):
        @pl.loop(0, LEAVES)
        def _(g):
            pts = sf[0, g] if d == 0 else sg[d, g]
            col = half_col(pts)
            for k in range(4):
                there, f = entry(d, g, k)
                row = norms[f][0:1] + jnp.where(there, 0.0, -1e30)
                inner = mm(pts, sf[f // LEAVES, f % LEAVES], NT)
                tiles[d, g, :, k * 128 : (k + 1) * 128] = kernel_exp(inner, col, row).astype(BF16)

    couple(2)
    couple(1)
    forward(q_ring, 6)
    couple(3)
    couple(0)

    for i in (5, 6):
        for way in (0, 1):
            q_ring[i][way].wait_recv()

    def partial(d, out):
        @pl.loop(0, LEAVES)
        def _(g):
            total = None
            for k in range(4):
                _, f = entry(d, g, k)
                term = mm(tiles[d, g, :, k * 128 : (k + 1) * 128], qf[f // LEAVES, f % LEAVES])
                total = term if total is None else total + term
            out(g, total)

    for d in (2, 1, 3):

        def put(g, total, d=d):
            h_out[d, g] = total.astype(BF16)

        partial(d, put)
        h_copies[d - 1].start()

    def put_own(g, total):
        h_own[g] = total

    partial(0, put_own)
    for copy in h_arrivals:
        copy.wait_recv()

    @pl.loop(0, LEAVES // 2)
    def _(i):
        for g in (2 * i, 2 * i + 1):
            total = h_own[g]
            for d in range(1, XN):
                total = total + h_in[d, g].astype(F32)
            value = near_sum[g] + mm(basis[g], total.astype(BF16))
            pot_ref[g] = value.astype(BF16)

    t_copy.wait_recv()
    other_copy = pltpu.make_async_copy(
        t_recv, transfer_ref.at[pl.ds(theirs, HALF)], local_sem.at[1 + XN]
    )
    other_copy.start()
    for copies in (*s_ring, *q_ring, x_copies, l_copies, h_copies, (pick_copy, sib_copy, t_copy)):
        for copy in copies:
            copy.wait_send()
    keep_copy.wait()
    other_copy.wait()


def body(points, charges, skel, near_list, far_gap, far_leaf, par_pick):
    x = points.reshape(LEAVES, 256, 128)
    c = charges.reshape(LEAVES, 256, 128)
    codes = (far_gap * LEAVES + far_leaf).reshape(1, 64)
    codes = jnp.pad(codes, ((0, 7), (0, 64)))
    pick = jnp.pad(par_pick, ((0, 0), (0, 64)))
    vmem = pl.BlockSpec(memory_space=pltpu.VMEM)
    smem = pl.BlockSpec(memory_space=pltpu.SMEM)
    block = (LEAVES, 128, 128)
    pot, transfer = pl.pallas_call(
        kernel,
        out_shape=(
            jax.ShapeDtypeStruct((LEAVES, 256, 128), BF16),
            jax.ShapeDtypeStruct((LEAVES, 128, 128), F32),
        ),
        in_specs=[vmem, vmem, vmem, smem, vmem, vmem],
        out_specs=(vmem, pl.BlockSpec(memory_space=pl.ANY)),
        scratch_shapes=[
            pltpu.VMEM((ZN, *block), BF16),
            pltpu.VMEM((ZN, *block), BF16),
            pltpu.VMEM((XN, *block), BF16),
            pltpu.VMEM((XN, 8, 128), jnp.int32),
            pltpu.SMEM((XN, 8, 128), jnp.int32),
            pltpu.VMEM((HALF, 128, 128), BF16),
            pltpu.VMEM((LEAVES, 128), jnp.int32),
            pltpu.VMEM((LEAVES, 256, 256), BF16),
            pltpu.VMEM((LEAVES, 256, 256), BF16),
            pltpu.VMEM((LEAVES, 256, 128), BF16),
            pltpu.VMEM((LEAVES, 256, 128), F32),
            pltpu.VMEM((ZN * LEAVES, 8, 128), F32),
            pltpu.VMEM((XN, LEAVES, 128, 512), BF16),
            pltpu.VMEM((XN, *block), BF16),
            pltpu.VMEM((XN, *block), BF16),
            pltpu.VMEM(block, F32),
            pltpu.VMEM((HALF, 128, 384), F32),
            pltpu.VMEM((HALF, 128, 128), F32),
            pltpu.VMEM((HALF, 128, 128), F32),
            pltpu.VMEM((HALF, 128, 128), F32),
            pltpu.SemaphoreType.DMA((2, CHUNKS)),
            pltpu.SemaphoreType.DMA((2, CHUNKS)),
            pltpu.SemaphoreType.DMA((2, CHUNKS)),
            pltpu.SemaphoreType.DMA((2, CHUNKS)),
            pltpu.SemaphoreType.DMA((XN,)),
            pltpu.SemaphoreType.DMA((XN,)),
            pltpu.SemaphoreType.DMA((XN,)),
            pltpu.SemaphoreType.DMA((XN,)),
            pltpu.SemaphoreType.DMA((XN,)),
            pltpu.SemaphoreType.DMA((XN,)),
            pltpu.SemaphoreType.DMA((3,)),
            pltpu.SemaphoreType.DMA((3,)),
            pltpu.SemaphoreType.DMA((2 + XN,)),
        ],
        compiler_params=pltpu.CompilerParams(
            collective_id=0, has_side_effects=True, vmem_limit_bytes=56 << 20
        ),
        cost_estimate=pl.CostEstimate(flops=5_000_000_000, bytes_accessed=5_000_000, transcendentals=10_000_000),
    )(x, c, skel, near_list, codes, pick)
    return pot.reshape(LEAVES * 256, 128), transfer


def solution(mesh):
    placed = P(("wide", "sib"), None)
    return jax.shard_map(
        body,
        mesh=mesh,
        in_specs=(placed,) * 7,
        out_specs=(placed, P(("wide", "sib"), None, None)),
        check_vma=False,
    )
```

time: 615 us -> 136 us (0.22)
  other arithmetic: 364 us -> 0.68 us
  Pallas kernels: 0 us -> 127 us
  waiting for transfers between devices: 106 us -> 0 us
  local copies, waits for them, and re-layouts: 67.5 us -> 6.05 us
  matrix products: 43.7 us -> 0 us
  starting transfers between devices: 30.8 us -> 0 us
    another operation x8 -> x0, other arithmetic: 348 us -> none  [the longest x4 189 us: body(): lower = jnp.linalg.cholesky(gram_sum)]
    pallas_call x0 -> x1, Pallas kernels: none -> 127 us  [body(): pl.pallas_call(kernel, out_shape=(jax.ShapeDtypeStruct((LEAVES, 256, 128)...]
    all_to_all x3 -> x0, waiting for transfers between devices: 106 us -> none  [the longest x1 106 us: body(): lax.all_to_all(skel_pts[asked_ids], 'wide', split_axis=0, concat_axis=0,...]
    gather x23 -> x0, local copies, waits for them, and re-layouts: 58.5 us -> none  [the longest x8 12.4 us: near_block(): leaf_chg[near_ids].reshape(pair_count, near_count * leaf_rows, target_cols)]
    dot_general x16 -> x0, matrix products: 41.5 us -> none  [the longest x8 24.7 us: near_block(): jnp.einsum('lpm,lmc->lpc', near_tiles, near_chg, preferred_element_type=j...]
    all_to_all x3 -> x0, starting transfers between devices: 30.3 us -> none  [the longest x1 11.6 us: body(): lax.all_to_all(wanted, 'wide', split_axis=0, concat_axis=0, tiled=True)]
    reduce_sum x21 -> x0, other arithmetic: 9.16 us -> none  [the longest x11 7.21 us: kernel_block(): right_sq = jnp.sum(right_wide * right_wide, axis=-1)]
  transfers between devices with their start and end apart: 5 -> 0, of which waited for: 1 -> 0; matrix products, arithmetic and copies ran while one was open for 73% -> 0% of each run, Pallas kernels for 0% -> 0%
where the time goes in v1:
time: 136 us; the launch traced here: 135 us
  Pallas kernels  127 us (93%)
  local copies, waits for them, and re-layouts  6.05 us (4%)
    pallas_call x1, Pallas kernels, body(): pl.pallas_call(kernel, out_shape=(jax.ShapeDtypeStruct((LEAVES, 256, 128)...  127 us
    unnamed x11, local copies, waits for them, and re-layouts  4.69 us

profile of v1, /device:TPU:14, one launch (start us, length us, event | category | flops | bytes accessed | tf_op | source)
XLA Modules:
  0.0 134.6 jit_solution(12548800108602798955)
XLA Ops:
  0.6 0.0 copy-start.3
  0.6 0.7 copy-done.3
  1.3 0.7 multiply_add_fusion
  2.0 0.1 copy.11
  2.1 0.0 copy-start.2
  2.1 0.1 reshape.18
  2.2 0.0 copy-start.1
  2.2 0.6 pad.8.codes_ref
  2.8 0.0 copy-done.2
  2.8 0.7 copy.12.near_ref
  3.5 0.0 copy-done.1
  3.5 0.6 pad.9.pick_ref
  4.1 127.2 %shard_map.86 = (bf16[16,256,128]{2,1,0:T(8,128)(2,1)}, f32[16,128,128]{2,1,0:T(8,128)}) custom-call(bf16[16,256,128]{2,1,0:T(8,128)(2,1)} %bitcast.4, bf16[16,256,128]{2,1,0:T(8,128)(2,1)} %bitcast.5, s32[16,128]{1,0:T(8,128)} %skel_ref.1, s32[16,6]{1,0:T(8,128)} %copy.12.near_ref, s32[8,128]{1,0:T(8,128)} %pad.8.codes_ref, s32[16,128]{1,0:T(8,128)} %pad.9.pick_ref), custom_call_target="tpu_custom_call" | custom-call | flops 5000000000 | bytes 5000000 | tf_op jit(solution)/shard_map/pallas_call | solution.py:417
  131.2 0.0 copy-start
  131.2 2.4 %copy.15 = bf16[4096,128]{1,0:T(8,128)(2,1)} copy(bf16[4096,128]{1,0:T(8,128)(2,1)} %bitcast.3) | data formatting | bytes 2097152
  133.6 0.0 copy-done
  133.6 1.0 copy.16
Async XLA Ops:
  0.6 0.7 copy-start.3
  2.1 0.7 copy-start.2
  2.2 1.3 copy-start.1
  131.2 2.4 %copy-start = (f32[16,128,128]{2,1,0:T(8,128)S(1)}, f32[16,128,128]{2,1,0:T(8,128)}, u32[]{:S(2)}) copy-start(f32[16,128,128]{2,1,0:T(8,128)} %get-tuple-element.9) | copy-start | bytes 3145732

commit v2 on v1

--- a/solution.py
+++ b/solution.py
@@ -19,6 +19,7 @@
 XN, ZN = 4, 8
 PANEL = 32
 CHUNKS = 7
+PARTS, STARTS, COLS = 2, (0, 64), (64, 64)
 UP = [(0, 0), (0, 1), (7, 0), (7, 1), (6, 0), (6, 1), (5, 0)]
 DOWN = [(0, 1), (0, 0), (1, 1), (1, 0), (2, 1), (2, 0), (3, 1)]
 
@@ -142,9 +143,9 @@
     x_ref, c_ref, skel_ref, near_ref, codes_ref, pick_ref,
     pot_ref, transfer_ref,
     sf, qf, sg, lists, list_sm, sib_s, sib_pick, left, right, basis, near_sum,
-    norms, tiles, h_out, h_in, h_own, w, t_keep, t_send, t_recv,
-    s_send, s_recv, q_send, q_recv, x_send, x_recv, h_send, h_recv,
-    l_send, l_recv, b_send, b_recv, local_sem,
+    norms, tiles, h_out, h_far, h_in, h_own, w, t_send, t_recv,
+    s_send, s_recv, q_send, q_recv, n_send, n_recv, x_send, x_recv, f_send, f_recv,
+    h_send, h_recv, l_send, l_recv, b_send, b_recv, local_sem,
 ):
     wide, sib = lax.axis_index("wide"), lax.axis_index("sib")
     x, z = wide // ZN, wide % ZN
@@ -179,7 +180,21 @@
             pairs.append(pair)
         return pairs
 
-    s_ring, q_ring = ring(sf, s_send, s_recv), ring(qf, q_send, q_recv)
+    s_ring = ring(sf, s_send, s_recv)
+    q_ring = [ring(qf[p], q_send.at[p], q_recv.at[p]) for p in range(PARTS)]
+    n_ring = []
+    for hop in range(4):
+        up, down = (ZN - hop) % ZN, hop
+        pair = [
+            remote(norms.at[up], norms.at[up - 1 if hop else ZN - 1],
+                   n_send.at[0, hop], n_recv.at[0, hop], above)
+        ]
+        if hop < 3:
+            pair.append(
+                remote(norms.at[down], norms.at[down + 1],
+                       n_send.at[1, hop], n_recv.at[1, hop], below)
+            )
+        n_ring.append(pair)
     x_copies = [
         remote(sf.at[0], sg.at[XN - d], x_send.at[d], x_recv.at[XN - d], peers[d])
         for d in range(1, XN)
@@ -194,22 +209,39 @@
     l_arrivals = [
         remote(codes_ref, lists.at[d], l_send.at[d], l_recv.at[d], peers[d]) for d in range(1, XN)
     ]
+    f_copies = [
+        [
+            remote(h_out[p].at[2, pl.ds(way * HALF, HALF)], h_far[p].at[way],
+                   f_send.at[p, way], f_recv.at[p, way], peers[1 + 2 * way])
+            for way in (0, 1)
+        ]
+        for p in range(PARTS)
+    ]
     h_copies = [
-        remote(h_out.at[d], h_in.at[XN - d], h_send.at[d], h_recv.at[XN - d], peers[d])
-        for d in range(1, XN)
-    ]
-    h_arrivals = [
-        remote(h_out.at[d], h_in.at[d], h_send.at[d], h_recv.at[d], peers[d]) for d in range(1, XN)
+        [
+            remote(h_out[p].at[1 + 2 * way], h_in[p].at[way],
+                   h_send.at[p, way], h_recv.at[p, way], peers[1 + 2 * way])
+            for way in (0, 1)
+        ]
+        for p in range(PARTS)
     ]
     mine, theirs = odd * HALF, HALF - odd * HALF
     pick_copy = remote(pick_ref, sib_pick, b_send.at[0], b_recv.at[0], twin)
     sib_copy = remote(sf.at[0, pl.ds(theirs, HALF)], sib_s, b_send.at[1], b_recv.at[1], twin)
     t_copy = remote(t_send, t_recv, b_send.at[2], b_recv.at[2], twin)
 
-    def forward(copies, i):
-        for way in (0, 1):
-            copies[i - 2][way].wait_recv()
-            copies[i][way].start()
+    def start(copies, *chunks):
+        for i in chunks:
+            for way in (0, 1):
+                if i >= 2:
+                    copies[i - 2][way].wait_recv()
+                copies[i][way].start()
+
+    def start_norms(hop):
+        for way, copy in enumerate(n_ring[hop]):
+            if hop:
+                n_ring[hop - 1][way].wait_recv()
+            copy.start()
 
     def skeleton(g):
         sf[0, g] = pick_rows(skel_ref[pl.ds(g, 1), :], x_ref[g])
@@ -239,42 +271,43 @@
 
     def compress(g):
         pts, skel_pts = x_ref[g], sf[0, g]
-        block = kernel_exp(mm(pts, skel_pts, NT), half_col(pts), half_rows(skel_pts)[0:1])
-        block = block.astype(BF16)
+        row = half_rows(skel_pts)[0:1]
+        norms[0, pl.ds(g, 1), :] = row
+        block = kernel_exp(mm(pts, skel_pts, NT), half_col(pts), row).astype(BF16)
         basis[g] = block
-        qf[0, g] = mm(block, c_ref[g], TN).astype(BF16)
-
-    def bases(first, last):
-        @pl.loop(first // 2, last // 2)
-        def _(i):
-            compress(2 * i)
-            compress(2 * i + 1)
-
-    bases(0, 8)
-    forward(s_ring, 2)
-    bases(8, 16)
-    forward(s_ring, 3)
-    for i in (0, 1):
-        for way in (0, 1):
-            q_ring[i][way].start()
-
-    @pl.loop(0, LEAVES)
+        squeezed = mm(c_ref[g], block, TN).astype(BF16)
+        for p in range(PARTS):
+            qf[p][0, g] = squeezed[STARTS[p] : STARTS[p] + COLS[p]]
+
+    @pl.loop(0, LEAVES // 2, unroll=2)
+    def _(i):
+        compress(2 * i)
+        compress(2 * i + 1)
+
+    start(q_ring[0], 0, 1)
+    start_norms(0)
+
+    @pl.loop(0, LEAVES, unroll=4)
     def _(g):
         near_prepare(x_ref, left, right, g)
 
     def near(first, last):
-        @pl.loop(first, last)
+        @pl.loop(first, last, unroll=2)
         def _(g):
             near_sum[g] = near_leaf(left, right, c_ref, near_ref, g)
 
-    near(0, 4)
-    forward(s_ring, 4)
-    near(4, 8)
-    forward(q_ring, 2)
+    near(0, 6)
+    start(s_ring, 2)
+    near(6, 8)
+    start(s_ring, 3)
     near(8, 12)
-    forward(s_ring, 5)
-    near(12, 16)
-    forward(q_ring, 3)
+    start(q_ring[0], 2)
+    near(12, 14)
+    start(q_ring[0], 3)
+    start_norms(1)
+    near(14, 16)
+    start(s_ring, 4)
+    start(q_ring[1], 0, 1)
 
     pick_copy.wait_recv()
     sib_copy.wait_recv()
@@ -283,8 +316,8 @@
     def _(i):
         for m in (2 * i, 2 * i + 1):
             own, other = sf[0, mine + m], sib_s[m]
-            own_pick = pick_ref[pl.ds(mine + m, 1), 0:64]
-            other_pick = sib_pick[pl.ds(mine + m, 1), 0:64]
+            own_pick = pick_ref[pl.ds(mine + m, 1), :]
+            other_pick = sib_pick[pl.ds(mine + m, 1), :]
             build_parent(
                 w, m,
                 jnp.where(odd == 1, other, own), jnp.where(odd == 1, own, other),
@@ -292,117 +325,139 @@
                 jnp.where(odd == 1, own_pick, other_pick),
             )
 
-    forward(s_ring, 6)
+    start(s_ring, 5)
+    start_norms(2)
     factor_panel(w, 0)
-    forward(q_ring, 4)
+    start(q_ring[0], 4)
+    start(s_ring, 6)
+    start_norms(3)
     factor_panel(w, 1)
+    start(q_ring[0], 5)
+    start(q_ring[1], 2)
     factor_panel(w, 2)
-    forward(q_ring, 5)
+    start(q_ring[0], 6)
+    start(q_ring[1], 3)
     factor_panel(w, 3)
 
     @pl.loop(0, HALF)
     def _(m):
         ta = w[m, :, 128:256].T * 16.0
         tb = w[m, :, 256:384].T * 16.0
-        t_keep[m] = jnp.where(odd == 1, tb, ta)
+        transfer_ref[mine + m] = jnp.where(odd == 1, tb, ta)
         t_send[m] = jnp.where(odd == 1, ta, tb)
 
     t_copy.start()
-    keep_copy = pltpu.make_async_copy(t_keep, transfer_ref.at[pl.ds(mine, HALF)], local_sem.at[0])
-    keep_copy.start()
 
     for copy in l_arrivals:
         copy.wait_recv()
     list_copies = [
-        pltpu.make_async_copy(codes_ref if d == 0 else lists.at[d], list_sm.at[d], local_sem.at[1 + d])
+        pltpu.make_async_copy(codes_ref if d == 0 else lists.at[d], list_sm.at[d], local_sem.at[d])
         for d in range(XN)
     ]
     for copy in list_copies:
         copy.start()
-    for i in (5, 6):
-        for way in (0, 1):
-            s_ring[i][way].wait_recv()
-    for copy in x_arrivals:
+    for copy in (*s_ring[5], *s_ring[6], *x_arrivals, n_ring[2][1], n_ring[3][0]):
         copy.wait_recv()
     for copy in list_copies:
         copy.wait()
-
-    @pl.loop(0, ZN * LEAVES // 4)
-    def _(i):
-        for f in range(4):
-            norms[4 * i + f] = half_rows(sf[i // 4, i % 4 * 4 + f])
 
     def entry(d, g, k):
         code = list_sm[d, 0, g * 4 + k]
         ahead = 1 + (code >> 4)
         there = ((z + ahead >> 3) + d & XN - 1) == 0
-        return there, (ahead & ZN - 1) * LEAVES + (code & LEAVES - 1)
+        return there, ahead & ZN - 1, code & LEAVES - 1
 
     def couple(d):
-        @pl.loop(0, LEAVES)
+        @pl.loop(0, LEAVES, unroll=4)
         def _(g):
             pts = sf[0, g] if d == 0 else sg[d, g]
             col = half_col(pts)
+            rows, named = [], []
             for k in range(4):
-                there, f = entry(d, g, k)
-                row = norms[f][0:1] + jnp.where(there, 0.0, -1e30)
-                inner = mm(pts, sf[f // LEAVES, f % LEAVES], NT)
-                tiles[d, g, :, k * 128 : (k + 1) * 128] = kernel_exp(inner, col, row).astype(BF16)
+                there, slot, leaf = entry(d, g, k)
+                rows.append(norms[slot, pl.ds(leaf, 1), :] + jnp.where(there, 0.0, -1e30))
+                named.append(sf[slot, leaf])
+            inner = mm(pts, jnp.concatenate(named, axis=0), NT)
+            col = jnp.concatenate([col] * 4, axis=1)
+            tiles[d, g] = kernel_exp(inner, col, jnp.concatenate(rows, axis=1)).astype(BF16)
 
     couple(2)
+    start(q_ring[1], 4)
     couple(1)
-    forward(q_ring, 6)
+    start(q_ring[1], 5)
     couple(3)
     couple(0)
 
-    for i in (5, 6):
+    def partial(p, d, first, last, out):
+        @pl.loop(first, last, unroll=8)
+        def _(g):
+            named = []
+            for k in range(4):
+                _, slot, leaf = entry(d, g, k)
+                named.append(qf[p][slot, leaf])
+            out(g, mm(jnp.concatenate(named, axis=1), tiles[d, g], NT))
+
+    def far_part(p):
         for way in (0, 1):
-            q_ring[i][way].wait_recv()
-
-    def partial(d, out):
-        @pl.loop(0, LEAVES)
-        def _(g):
-            total = None
-            for k in range(4):
-                _, f = entry(d, g, k)
-                term = mm(tiles[d, g, :, k * 128 : (k + 1) * 128], qf[f // LEAVES, f % LEAVES])
-                total = term if total is None else total + term
-            out(g, total)
-
-    for d in (2, 1, 3):
-
-        def put(g, total, d=d):
-            h_out[d, g] = total.astype(BF16)
-
-        partial(d, put)
-        h_copies[d - 1].start()
-
-    def put_own(g, total):
-        h_own[g] = total
-
-    partial(0, put_own)
-    for copy in h_arrivals:
-        copy.wait_recv()
+            for i in (5, 6):
+                q_ring[p][i][way].wait_recv()
+
+        def put_far(g, total):
+            h_out[p][2, g] = total.astype(BF16)
+
+        def put_own(g, total):
+            h_own[p][g] = total
+
+        partial(p, 2, 0, LEAVES, put_far)
+        for way in (0, 1):
+            f_copies[p][way].start()
+        if p == 0:
+            start(q_ring[1], 6)
+        partial(p, 0, 0, LEAVES, put_own)
+        for way in (0, 1):
+            d = 1 + 2 * way
+
+            def put(g, total, d=d):
+                h_out[p][d, g] = total.astype(BF16)
+
+            def put_sum(g, total, d=d, way=way):
+                total = total + h_far[p][way, g - way * HALF].astype(F32)
+                h_out[p][d, g] = total.astype(BF16)
+
+            partial(p, d, HALF - way * HALF, LEAVES - way * HALF, put)
+            f_copies[p][way].wait_recv()
+            partial(p, d, way * HALF, HALF + way * HALF, put_sum)
+            h_copies[p][way].start()
+
+    far_part(0)
+
+    t_copy.wait_recv()
+
+    @pl.loop(0, HALF)
+    def _(m):
+        transfer_ref[theirs + m] = t_recv[m]
+
+    far_part(1)
+    for copies in h_copies:
+        for copy in copies:
+            copy.wait_recv()
 
     @pl.loop(0, LEAVES // 2)
     def _(i):
         for g in (2 * i, 2 * i + 1):
-            total = h_own[g]
-            for d in range(1, XN):
-                total = total + h_in[d, g].astype(F32)
-            value = near_sum[g] + mm(basis[g], total.astype(BF16))
+            total = []
+            for p in range(PARTS):
+                share = h_own[p][g] + h_in[p][0, g].astype(F32) + h_in[p][1, g].astype(F32)
+                total.append(share.astype(BF16))
+            value = near_sum[g] + mm(basis[g], jnp.concatenate(total, axis=0), NT)
             pot_ref[g] = value.astype(BF16)
 
-    t_copy.wait_recv()
-    other_copy = pltpu.make_async_copy(
-        t_recv, transfer_ref.at[pl.ds(theirs, HALF)], local_sem.at[1 + XN]
-    )
-    other_copy.start()
-    for copies in (*s_ring, *q_ring, x_copies, l_copies, h_copies, (pick_copy, sib_copy, t_copy)):
+    sent = [*s_ring, *n_ring, x_copies, l_copies, *f_copies, *h_copies]
+    for p in range(PARTS):
+        sent.extend(q_ring[p])
+    for copies in (*sent, (pick_copy, sib_copy, t_copy)):
         for copy in copies:
             copy.wait_send()
-    keep_copy.wait()
-    other_copy.wait()
 
 
 def body(points, charges, skel, near_list, far_gap, far_leaf, par_pick):
@@ -410,7 +465,6 @@
     c = charges.reshape(LEAVES, 256, 128)
     codes = (far_gap * LEAVES + far_leaf).reshape(1, 64)
     codes = jnp.pad(codes, ((0, 7), (0, 64)))
-    pick = jnp.pad(par_pick, ((0, 0), (0, 64)))
     vmem = pl.BlockSpec(memory_space=pltpu.VMEM)
     smem = pl.BlockSpec(memory_space=pltpu.SMEM)
     block = (LEAVES, 128, 128)
@@ -421,47 +475,51 @@
             jax.ShapeDtypeStruct((LEAVES, 128, 128), F32),
         ),
         in_specs=[vmem, vmem, vmem, smem, vmem, vmem],
-        out_specs=(vmem, pl.BlockSpec(memory_space=pl.ANY)),
+        out_specs=(vmem, vmem),
         scratch_shapes=[
             pltpu.VMEM((ZN, *block), BF16),
-            pltpu.VMEM((ZN, *block), BF16),
+            [pltpu.VMEM((ZN, LEAVES, n, 128), BF16) for n in COLS],
             pltpu.VMEM((XN, *block), BF16),
             pltpu.VMEM((XN, 8, 128), jnp.int32),
             pltpu.SMEM((XN, 8, 128), jnp.int32),
             pltpu.VMEM((HALF, 128, 128), BF16),
-            pltpu.VMEM((LEAVES, 128), jnp.int32),
+            pltpu.VMEM((LEAVES, 64), jnp.int32),
             pltpu.VMEM((LEAVES, 256, 256), BF16),
             pltpu.VMEM((LEAVES, 256, 256), BF16),
             pltpu.VMEM((LEAVES, 256, 128), BF16),
             pltpu.VMEM((LEAVES, 256, 128), F32),
-            pltpu.VMEM((ZN * LEAVES, 8, 128), F32),
+            pltpu.VMEM((ZN, LEAVES, 128), F32),
             pltpu.VMEM((XN, LEAVES, 128, 512), BF16),
-            pltpu.VMEM((XN, *block), BF16),
-            pltpu.VMEM((XN, *block), BF16),
-            pltpu.VMEM(block, F32),
+            [pltpu.VMEM((XN, LEAVES, n, 128), BF16) for n in COLS],
+            [pltpu.VMEM((2, HALF, n, 128), BF16) for n in COLS],
+            [pltpu.VMEM((2, LEAVES, n, 128), BF16) for n in COLS],
+            [pltpu.VMEM((LEAVES, n, 128), F32) for n in COLS],
             pltpu.VMEM((HALF, 128, 384), F32),
-            pltpu.VMEM((HALF, 128, 128), F32),
             pltpu.VMEM((HALF, 128, 128), F32),
             pltpu.VMEM((HALF, 128, 128), F32),
             pltpu.SemaphoreType.DMA((2, CHUNKS)),
             pltpu.SemaphoreType.DMA((2, CHUNKS)),
-            pltpu.SemaphoreType.DMA((2, CHUNKS)),
-            pltpu.SemaphoreType.DMA((2, CHUNKS)),
+            pltpu.SemaphoreType.DMA((PARTS, 2, CHUNKS)),
+            pltpu.SemaphoreType.DMA((PARTS, 2, CHUNKS)),
+            pltpu.SemaphoreType.DMA((2, 4)),
+            pltpu.SemaphoreType.DMA((2, 4)),
             pltpu.SemaphoreType.DMA((XN,)),
             pltpu.SemaphoreType.DMA((XN,)),
-            pltpu.SemaphoreType.DMA((XN,)),
-            pltpu.SemaphoreType.DMA((XN,)),
+            pltpu.SemaphoreType.DMA((PARTS, 2)),
+            pltpu.SemaphoreType.DMA((PARTS, 2)),
+            pltpu.SemaphoreType.DMA((PARTS, 2)),
+            pltpu.SemaphoreType.DMA((PARTS, 2)),
             pltpu.SemaphoreType.DMA((XN,)),
             pltpu.SemaphoreType.DMA((XN,)),
             pltpu.SemaphoreType.DMA((3,)),
             pltpu.SemaphoreType.DMA((3,)),
-            pltpu.SemaphoreType.DMA((2 + XN,)),
+            pltpu.SemaphoreType.DMA((XN,)),
         ],
         compiler_params=pltpu.CompilerParams(
             collective_id=0, has_side_effects=True, vmem_limit_bytes=56 << 20
         ),
         cost_estimate=pl.CostEstimate(flops=5_000_000_000, bytes_accessed=5_000_000, transcendentals=10_000_000),
-    )(x, c, skel, near_list, codes, pick)
+    )(x, c, skel, near_list, codes, par_pick)
     return pot.reshape(LEAVES * 256, 128), transfer
 
 

time: 136 us -> 119 us (0.88)
  Pallas kernels: 127 us -> 112 us
    pallas_call x1, Pallas kernels: 127 us -> 112 us  [body(): pl.pallas_call(kernel, out_shape=(jax.ShapeDtypeStruct((LEAVES, 256, 128)...]
    unnamed x11 -> x9, local copies, waits for them, and re-layouts: 4.69 us -> 4.76 us
where the time goes in v2:
time: 119 us
  Pallas kernels  112 us (94%)
  local copies, waits for them, and re-layouts  5.53 us (5%)
    pallas_call x1, Pallas kernels, body(): pl.pallas_call(kernel, out_shape=(jax.ShapeDtypeStruct((LEAVES, 256, 128)...  112 us
    unnamed x9, local copies, waits for them, and re-layouts  4.76 us

profile of v2, /device:TPU:14, one launch (start us, length us, event | category | flops | bytes accessed | tf_op | source)
XLA Modules:
  0.0 118.9 jit_solution(9083765169830596853)
XLA Ops:
  0.6 0.0 copy-start.2
  0.6 0.7 copy-done.2
  1.3 0.7 multiply_add_fusion
  2.0 0.1 copy.11
  2.1 0.1 reshape.18
  2.2 0.0 copy-start.1
  2.2 0.6 pad.4.codes_ref
  2.8 0.1 copy-done.1
  2.9 0.7 copy.12.near_ref
  3.5 112.0 %shard_map.86 = (bf16[16,256,128]{2,1,0:T(8,128)(2,1)}, f32[16,128,128]{2,1,0:T(8,128)}) custom-call(bf16[16,256,128]{2,1,0:T(8,128)(2,1)} %bitcast.4, bf16[16,256,128]{2,1,0:T(8,128)(2,1)} %bitcast.5, s32[16,128]{1,0:T(8,128)} %skel_ref.1, s32[16,6]{1,0:T(8,128)} %copy.12.near_ref, s32[8,128]{1,0:T(8,128)} %pad.4.codes_ref, s32[16,64]{1,0:T(8,128)} %pick_ref.1), custom_call_target="tpu_custom_call" | custom-call | flops 5000000000 | bytes 5000000 | tf_op jit(solution)/shard_map/pallas_call | solution.py:471
  115.5 0.0 copy-start
  115.5 2.4 %copy.15 = bf16[4096,128]{1,0:T(8,128)(2,1)} copy(bf16[4096,128]{1,0:T(8,128)(2,1)} %bitcast.3) | data formatting | bytes 2097152
  117.9 0.0 copy-done
  117.9 1.0 copy.16
Async XLA Ops:
  0.6 0.7 copy-start.2
  2.2 0.7 copy-start.1
  115.5 2.4 %copy-start = (f32[16,128,128]{2,1,0:T(8,128)S(1)}, f32[16,128,128]{2,1,0:T(8,128)}, u32[]{:S(2)}) copy-start(f32[16,128,128]{2,1,0:T(8,128)} %get-tuple-element.9) | copy-start | bytes 3145732

commit v3 on v2

--- a/solution.py
+++ b/solution.py
@@ -219,9 +219,11 @@
     ]
     h_copies = [
         [
-            remote(h_out[p].at[1 + 2 * way], h_in[p].at[way],
-                   h_send.at[p, way], h_recv.at[p, way], peers[1 + 2 * way])
+            remote(h_out[p].at[1 + 2 * way, pl.ds(half * HALF, HALF)],
+                   h_in[p].at[way, pl.ds(half * HALF, HALF)],
+                   h_send.at[p, way, half], h_recv.at[p, way, half], peers[1 + 2 * way])
             for way in (0, 1)
+            for half in (0, 1)
         ]
         for p in range(PARTS)
     ]
@@ -413,21 +415,25 @@
             f_copies[p][way].start()
         if p == 0:
             start(q_ring[1], 6)
+        for way in (0, 1):
+            d = 1 + 2 * way
+
+            def put(g, total, d=d):
+                h_out[p][d, g] = total.astype(BF16)
+
+            partial(p, d, HALF - way * HALF, LEAVES - way * HALF, put)
+            h_copies[p][way * 2 + 1 - way].start()
         partial(p, 0, 0, LEAVES, put_own)
         for way in (0, 1):
             d = 1 + 2 * way
 
-            def put(g, total, d=d):
-                h_out[p][d, g] = total.astype(BF16)
-
             def put_sum(g, total, d=d, way=way):
                 total = total + h_far[p][way, g - way * HALF].astype(F32)
                 h_out[p][d, g] = total.astype(BF16)
 
-            partial(p, d, HALF - way * HALF, LEAVES - way * HALF, put)
             f_copies[p][way].wait_recv()
             partial(p, d, way * HALF, HALF + way * HALF, put_sum)
-            h_copies[p][way].start()
+            h_copies[p][way * 2 + way].start()
 
     far_part(0)
 
@@ -507,8 +513,8 @@
             pltpu.SemaphoreType.DMA((XN,)),
             pltpu.SemaphoreType.DMA((PARTS, 2)),
             pltpu.SemaphoreType.DMA((PARTS, 2)),
-            pltpu.SemaphoreType.DMA((PARTS, 2)),
-            pltpu.SemaphoreType.DMA((PARTS, 2)),
+            pltpu.SemaphoreType.DMA((PARTS, 2, 2)),
+            pltpu.SemaphoreType.DMA((PARTS, 2, 2)),
             pltpu.SemaphoreType.DMA((XN,)),
             pltpu.SemaphoreType.DMA((XN,)),
             pltpu.SemaphoreType.DMA((3,)),

time: 119 us -> 118 us (level)
  Pallas kernels: 112 us -> 110 us
    pallas_call x1, Pallas kernels: 112 us -> 110 us  [body(): pl.pallas_call(kernel, out_shape=(jax.ShapeDtypeStruct((LEAVES, 256, 128)...]
where the time goes in v3:
time: 118 us; the launch traced here: 117 us
  Pallas kernels  110 us (93%)
  local copies, waits for them, and re-layouts  5.53 us (5%)
    pallas_call x1, Pallas kernels, body(): pl.pallas_call(kernel, out_shape=(jax.ShapeDtypeStruct((LEAVES, 256, 128)...  110 us
    unnamed x9, local copies, waits for them, and re-layouts  4.76 us

profile of v3, /device:TPU:14, one launch (start us, length us, event | category | flops | bytes accessed | tf_op | source)
XLA Modules:
  0.0 116.8 jit_solution(799102900444464867)
XLA Ops:
  0.6 0.0 copy-start.2
  0.6 0.7 copy-done.2
  1.3 0.7 multiply_add_fusion
  2.0 0.1 copy.11
  2.1 0.1 reshape.18
  2.2 0.0 copy-start.1
  2.2 0.6 pad.4.codes_ref
  2.8 0.1 copy-done.1
  2.9 0.7 copy.12.near_ref
  3.5 109.9 %shard_map.86 = (bf16[16,256,128]{2,1,0:T(8,128)(2,1)}, f32[16,128,128]{2,1,0:T(8,128)}) custom-call(bf16[16,256,128]{2,1,0:T(8,128)(2,1)} %bitcast.4, bf16[16,256,128]{2,1,0:T(8,128)(2,1)} %bitcast.5, s32[16,128]{1,0:T(8,128)} %skel_ref.1, s32[16,6]{1,0:T(8,128)} %copy.12.near_ref, s32[8,128]{1,0:T(8,128)} %pad.4.codes_ref, s32[16,64]{1,0:T(8,128)} %pick_ref.1), custom_call_target="tpu_custom_call" | custom-call | flops 5000000000 | bytes 5000000 | tf_op jit(solution)/shard_map/pallas_call | solution.py:477
  113.4 0.0 copy-start
  113.5 2.4 %copy.15 = bf16[4096,128]{1,0:T(8,128)(2,1)} copy(bf16[4096,128]{1,0:T(8,128)(2,1)} %bitcast.3) | data formatting | bytes 2097152
  115.8 0.0 copy-done
  115.8 1.0 copy.16
Async XLA Ops:
  0.6 0.7 copy-start.2
  2.2 0.7 copy-start.1
  113.4 2.4 %copy-start = (f32[16,128,128]{2,1,0:T(8,128)S(1)}, f32[16,128,128]{2,1,0:T(8,128)}, u32[]{:S(2)}) copy-start(f32[16,128,128]{2,1,0:T(8,128)} %get-tuple-element.9) | copy-start | bytes 3145732

commit v4 on v3

--- a/solution.py
+++ b/solution.py
@@ -140,9 +140,9 @@
 
 
 def kernel(
-    x_ref, c_ref, skel_ref, near_ref, codes_ref, pick_ref,
+    x_ref, c_ref, skel_ref, near_ref, gap_ref, leaf_ref, pick_ref,
     pot_ref, transfer_ref,
-    sf, qf, sg, lists, list_sm, sib_s, sib_pick, left, right, basis, near_sum,
+    sf, qf, sg, codes_ref, lists, list_sm, sib_s, sib_pick, left, right, basis, near_sum,
     norms, tiles, h_out, h_far, h_in, h_own, w, t_send, t_recv,
     s_send, s_recv, q_send, q_recv, n_send, n_recv, x_send, x_recv, f_send, f_recv,
     h_send, h_recv, l_send, l_recv, b_send, b_recv, local_sem,
@@ -253,6 +253,8 @@
         skeleton(2 * i)
         skeleton(2 * i + 1)
 
+    codes_ref[...] = jnp.zeros_like(codes_ref)
+    codes_ref[:, 0:4] = gap_ref[...] * LEAVES + leaf_ref[...]
     pl.semaphore_wait(barrier, 6)
     s_ring[0][0].start()
     s_ring[1][1].start()
@@ -364,7 +366,7 @@
         copy.wait()
 
     def entry(d, g, k):
-        code = list_sm[d, 0, g * 4 + k]
+        code = list_sm[d, g, k]
         ahead = 1 + (code >> 4)
         there = ((z + ahead >> 3) + d & XN - 1) == 0
         return there, ahead & ZN - 1, code & LEAVES - 1
@@ -469,8 +471,6 @@
 def body(points, charges, skel, near_list, far_gap, far_leaf, par_pick):
     x = points.reshape(LEAVES, 256, 128)
     c = charges.reshape(LEAVES, 256, 128)
-    codes = (far_gap * LEAVES + far_leaf).reshape(1, 64)
-    codes = jnp.pad(codes, ((0, 7), (0, 64)))
     vmem = pl.BlockSpec(memory_space=pltpu.VMEM)
     smem = pl.BlockSpec(memory_space=pltpu.SMEM)
     block = (LEAVES, 128, 128)
@@ -480,14 +480,15 @@
             jax.ShapeDtypeStruct((LEAVES, 256, 128), BF16),
             jax.ShapeDtypeStruct((LEAVES, 128, 128), F32),
         ),
-        in_specs=[vmem, vmem, vmem, smem, vmem, vmem],
+        in_specs=[vmem, vmem, vmem, smem, vmem, vmem, vmem],
         out_specs=(vmem, vmem),
         scratch_shapes=[
             pltpu.VMEM((ZN, *block), BF16),
             [pltpu.VMEM((ZN, LEAVES, n, 128), BF16) for n in COLS],
             pltpu.VMEM((XN, *block), BF16),
-            pltpu.VMEM((XN, 8, 128), jnp.int32),
-            pltpu.SMEM((XN, 8, 128), jnp.int32),
+            pltpu.VMEM((LEAVES, 128), jnp.int32),
+            pltpu.VMEM((XN, LEAVES, 128), jnp.int32),
+            pltpu.SMEM((XN, LEAVES, 128), jnp.int32),
             pltpu.VMEM((HALF, 128, 128), BF16),
             pltpu.VMEM((LEAVES, 64), jnp.int32),
             pltpu.VMEM((LEAVES, 256, 256), BF16),
@@ -525,7 +526,7 @@
             collective_id=0, has_side_effects=True, vmem_limit_bytes=56 << 20
         ),
         cost_estimate=pl.CostEstimate(flops=5_000_000_000, bytes_accessed=5_000_000, transcendentals=10_000_000),
-    )(x, c, skel, near_list, codes, par_pick)
+    )(x, c, skel, near_list, far_gap, far_leaf, par_pick)
     return pot.reshape(LEAVES * 256, 128), transfer
 
 

time: 118 us -> 117 us (level)
    unnamed x9 -> x11, local copies, waits for them, and re-layouts: 4.76 us -> 6.06 us
where the time goes in v4:
time: 117 us
  Pallas kernels  110 us (94%)
  local copies, waits for them, and re-layouts  6.06 us (5%)
    pallas_call x1, Pallas kernels, body(): pl.pallas_call(kernel, out_shape=(jax.ShapeDtypeStruct((LEAVES, 256, 128)...  110 us
    unnamed x11, local copies, waits for them, and re-layouts  6.06 us

profile of v4, /device:TPU:14, one launch (start us, length us, event | category | flops | bytes accessed | tf_op | source)
XLA Modules:
  0.0 116.6 jit_solution(3570196725459731745)
XLA Ops:
  0.6 0.0 copy-start.1
  0.6 1.4 %copy.9.near_ref = s32[16,6]{1,0:T(8,128)} copy(s32[16,6]{0,1:T(8,128)} %param.10) | data formatting | bytes 768 | tf_op args[3]
  2.0 0.0 copy-done.1
  2.0 0.0 copy-start.2
  2.0 0.7 copy.10.gap_ref
  2.7 0.0 copy-done.2
  2.7 0.7 copy.11.leaf_ref
  3.4 109.9 %shard_map.86 = (bf16[16,256,128]{2,1,0:T(8,128)(2,1)}, f32[16,128,128]{2,1,0:T(8,128)}) custom-call(bf16[16,256,128]{2,1,0:T(8,128)(2,1)} %bitcast.4, bf16[16,256,128]{2,1,0:T(8,128)(2,1)} %bitcast.5, s32[16,128]{1,0:T(8,128)} %skel_ref.1, s32[16,6]{1,0:T(8,128)} %copy.9.near_ref, s32[16,4]{1,0:T(8,128)} %copy.10.gap_ref, s32[16,4]{1,0:T(8,128)} %copy.11.leaf_ref, ...), custom_call_target="tpu_custom_call" | custom-call | flops 5000000000 | bytes 5000000 | tf_op jit(solution)/shard_map/pallas_call | solution.py:477
  113.3 0.0 copy-start
  113.3 2.4 %copy.14 = bf16[4096,128]{1,0:T(8,128)(2,1)} copy(bf16[4096,128]{1,0:T(8,128)(2,1)} %bitcast.3) | data formatting | bytes 2097152
  115.6 0.0 copy-done
  115.6 1.0 copy.15
Async XLA Ops:
  0.6 1.4 %copy-start.1 = (s32[16,4]{0,1:T(4,128)S(1)}, s32[16,4]{0,1:T(4,128)}, u32[]{:S(2)}) copy-start(s32[16,4]{0,1:T(4,128)} %param.11) | copy-start | bytes 772
  2.0 0.7 copy-start.2
  113.3 2.4 %copy-start = (f32[16,128,128]{2,1,0:T(8,128)S(1)}, f32[16,128,128]{2,1,0:T(8,128)}, u32[]{:S(2)}) copy-start(f32[16,128,128]{2,1,0:T(8,128)} %get-tuple-element.9) | copy-start | bytes 3145732
